TPU v7x, 512 devices: a whole 4x4x16 slice. The times are simulated.
512 devices in a mesh: dp: 128 (over z, y, core), head: 4 (over x).
Axes of the slice: x: 4, y: 4, z: 16, core: 2. Of those that a mesh axis runs over, the one named last changes fastest.
Arguments:
- tile_features: bfloat16 [45056, 768], P('dp')
- tile_weight: bfloat16 [768, 768], replicated, may hold values from -0.21875 to 0.21875
- tile_bias: float32 [768], replicated, may hold values from -3 to 3
- query_weight: bfloat16 [768, 768], P(None, 'head'), may hold values from -1.25 to 1.25
- key_weight: bfloat16 [768, 768], P(None, 'head'), may hold values from -0.21875 to 0.21875
- value_weight: bfloat16 [768, 768], P(None, 'head'), may hold values from -0.21875 to 0.21875
- output_weight: bfloat16 [768, 768], P('head'), may hold values from -0.21875 to 0.21875
- tile_region: int32 [45056], replicated, may hold values from 0 to 255, as said below
- region_block: int32 [256], replicated, may hold values from 0 to 255, as said below
- region_count: int32 [256], replicated, may hold values from 96 to 256, as said below
Outputs:
- tile_mixed: bfloat16 [256, 256, 768], P('dp', None, 'head')
- region_out: bfloat16 [256, 768], P('dp', 'head')
Inputs may be any that keep to these rules, and one draw needn't show every extreme that they name: region_block is a permutation of the blocks. region_count[r] is the number of tiles t with tile_region[t] = r; one index of dp holds at most 2 tiles of one region, and some region reaches it on every index. `tile_region`: each region has 96 to 256 tiles.
All inputs are finite; a program needn't handle non-finite values.
Results may differ from a plain program's by a relative error of at most 0.018.
The roundings to bfloat16 on the way count: a program that leaves them out, or rounds other values in their place, can miss the bound.
Values may be sent and summed in bfloat16 or wider, within the bound.
A program may use at most 64 MiB of HBM per device.

v0:
```python
import jax
import jax.numpy as jnp
from jax import lax
from jax.sharding import PartitionSpec as P

D = 768
HEADS = 12
SLOTS = 256
REG_DEV = 2


def tile_ranks(local_regions):
    count = local_regions.shape[0]
    order = lax.iota(jnp.int32, count)
    same = local_regions[:, None] == local_regions[None, :]
    earlier = order[None, :] < order[:, None]
    return jnp.sum((same & earlier).astype(jnp.int32), axis=1)


def embed(rows, tile_weight, tile_bias):
    hidden = jnp.dot(rows, tile_weight, preferred_element_type=jnp.float32) + tile_bias
    return jax.nn.gelu(hidden, approximate=True).astype(jnp.bfloat16)


def full_embedding(tile_features, tile_weight, tile_bias):
    return embed(tile_features, tile_weight, tile_bias)


def regroup_order(received, per_block, width):
    shards = received.shape[0]
    sectioned = received.reshape(shards, per_block, SLOTS // shards, width)
    return sectioned.transpose(1, 0, 2, 3).reshape(per_block, SLOTS, width)


def project(rows, weight):
    return jnp.dot(rows, weight, preferred_element_type=jnp.float32).astype(jnp.bfloat16)


def attend(queries, keys_in, vals_in, live, head_size):
    blocks, slot_count, width = queries.shape
    heads_here = width // head_size
    shape = (blocks, slot_count, heads_here, head_size)
    scores = jnp.einsum(
        "rqhe,rkhe->rhqk",
        queries.reshape(shape),
        keys_in.reshape(shape),
        preferred_element_type=jnp.float32,
    ) * head_size ** (-0.5)
    scores = jnp.where(live[:, None, None, :], scores, -1e30)
    top = jnp.max(scores, axis=-1, keepdims=True)
    weights = jnp.exp(scores - top)
    weights = (weights / jnp.sum(weights, axis=-1, keepdims=True)).astype(jnp.bfloat16)
    mixed = jnp.einsum(
        "rhqk,rkhe->rqhe", weights, vals_in.reshape(shape), preferred_element_type=jnp.float32
    )
    mixed = jnp.where(live[:, :, None, None], mixed, 0.0)
    return mixed.reshape(blocks, slot_count, width).astype(jnp.bfloat16)


def local(
    tile_features,
    tile_weight,
    tile_bias,
    query_weight,
    key_weight,
    value_weight,
    output_weight,
    tile_region,
    region_block,
    region_count,
):
    shards = lax.axis_size("dp")
    position = lax.axis_index("dp")
    tile_here = tile_features.shape[0]
    width = tile_features.shape[1]
    per_shard = SLOTS // shards
    head_size = D // HEADS
    local_regions = lax.dynamic_slice_in_dim(tile_region, position * tile_here, tile_here, 0)
    region_ids = lax.iota(jnp.int32, region_block.shape[0])
    matches = local_regions[:, None] == region_ids[None, :]
    local_blocks = jnp.sum(jnp.where(matches, region_block[None, :], 0), axis=1)
    flat = local_blocks * per_shard + tile_ranks(local_regions)
    slot_total = REG_DEV * SLOTS
    slot_tile = jnp.full((slot_total,), -1, jnp.int32).at[flat].set(lax.iota(jnp.int32, tile_here))
    occupied = slot_tile >= 0
    picked = jnp.maximum(slot_tile, 0)
    targets = position * REG_DEV + lax.iota(jnp.int32, REG_DEV)
    owned = region_block[:, None] == targets[None, :]
    owned_region = jnp.sum(jnp.where(owned, region_ids[:, None], 0), axis=0)
    owned_count = jnp.sum(jnp.where(owned, region_count[:, None], 0), axis=0).astype(jnp.float32)
    per_source = tile_region.reshape(shards, tile_here)
    held = jnp.sum(
        (per_source[:, :, None] == owned_region[None, None, :]).astype(jnp.int32), axis=1
    )
    live = lax.iota(jnp.int32, per_shard)[None, None, :] < held[:, :, None]
    live = live.transpose(1, 0, 2).reshape(REG_DEV, SLOTS)
    cols = query_weight.shape[1]
    embedded = full_embedding(tile_features, tile_weight, tile_bias)
    taken = jnp.where(occupied[:, None], embedded[picked], jnp.zeros((), embedded.dtype))
    received = lax.all_to_all(
        taken.reshape(shards, REG_DEV * per_shard, embedded.shape[1]),
        "dp",
        split_axis=0,
        concat_axis=0,
        tiled=True,
    )
    slotted = regroup_order(received, REG_DEV, width).reshape(slot_total, width)
    queries = project(slotted, query_weight).reshape(REG_DEV, SLOTS, cols)
    keys_in = project(slotted, key_weight).reshape(REG_DEV, SLOTS, cols)
    vals_in = project(slotted, value_weight).reshape(REG_DEV, SLOTS, cols)
    tile_mixed = attend(queries, keys_in, vals_in, live, head_size)
    pooled = (jnp.sum(tile_mixed.astype(jnp.float32), axis=1) / owned_count[:, None]).astype(
        jnp.bfloat16
    )
    partial_value = jnp.dot(pooled, output_weight, preferred_element_type=jnp.float32)
    region_out = lax.psum_scatter(partial_value, "head", scatter_dimension=1, tiled=True).astype(
        jnp.bfloat16
    )
    return (tile_mixed, region_out)


def solution(mesh):
    in_specs = (
        P("dp", None),
        P(),
        P(),
        P(None, "head"),
        P(None, "head"),
        P(None, "head"),
        P("head", None),
        P(),
        P(),
        P(),
    )
    out_specs = (P("dp", None, "head"), P("dp", "head"))
    return jax.shard_map(local, mesh=mesh, in_specs=in_specs, out_specs=out_specs, check_vma=False)
```

profile of v0, /device:TPU:1, one launch (start us, length us, event | category | flops | bytes accessed | tf_op | source)
XLA Modules:
  0.0 115.7 jit_solution(9267138438100380810)
XLA Ops:
  7.2 0.0 copy-start
  7.2 0.9 dynamic_slice.3
  8.1 0.2 convert_reduce_fusion
  8.3 0.9 select_reduce_fusion
  9.2 2.9 %scatter_custom_fusion = s32[512]{0:T(512)S(1)} fusion(s32[352]{0:T(512)S(1)} %fusion.22, s32[352]{0:T(512)S(1)} %iota.28, s32[]{:T(128)} %constant.3.clone.1), kind=kCustom, calls=%fused_computation.46 | custom fusion | bytes 2052 | tf_op jit(solution)/shard_map/scatter | solution.py:84
  12.2 0.1 broadcast_in_dim.100
  12.3 0.0 copy-done
  12.3 1.8 %fusion.11 = bf16[352,768]{1,0:T(8,128)(2,1)S(1)} fusion(bf16[352,768]{1,0:T(8,128)(2,1)} %param.10, bf16[768,768]{1,0:T(8,128)(2,1)S(1)} %copy-done, f32[768]{0:T(1024)} %param.12), kind=kOutput, calls=%fused_computation.22 | convolution fusion | flops 417939456 | bytes 2264064 | tf_op jit(solution)/shard_map/dot_general | solution.py:21
  14.1 2.0 %gather_fusion = bf16[512,768]{1,0:T(8,128)(2,1)S(1)} fusion(bf16[352,768]{1,0:T(8,128)(2,1)S(1)} %fusion.11, s32[1024]{0:T(1024)S(1)} %pad_clamp_fusion), kind=kCustom, calls=%fused_computation | custom fusion | bytes 1574912 | tf_op jit(solution)/shard_map/gather | solution.py:99
  16.2 0.2 gather.6
  16.4 1.3 %broadcast_select_fusion = bf16[128,4,768]{2,1,0:T(4,128)(2,1)} fusion(bf16[128,4,768]{2,1,0:T(4,128)(2,1)S(1)} %gather.6, pred[128,4]{1,0:T(8,128)(4,1)S(1)} %broadcast_in_dim.100), kind=kLoop, calls=%fused_computation.23 | loop fusion | flops 393216 | bytes 1573376 | tf_op jit(solution)/shard_map/jit(_where)/select_n | solution.py:99
  17.7 0.0 copy-start.5
  17.7 0.0 copy-start.6
  17.7 0.0 copy-start.7
  17.7 20.7 %all-to-all-start = ((bf16[128,4,768]{2,1,0:T(4,128)(2,1)}), bf16[128,4,768]{2,1,0:T(4,128)(2,1)S(1)}, u32[]{:S(2)}, u32[]{:S(2)}) async-start(bf16[128,4,768]{2,1,0:T(4,128)(2,1)} %broadcast_select_fusion), calls=%async_computation | async-start | bytes 1572864 | tf_op jit(solution)/shard_map/all_to_all | solution.py:100
  38.4 0.0 reduce-scatter.4.cloned.1.call-start
  38.5 0.0 copy-done.5
  38.5 0.1 eq.26
  38.6 0.0 copy-done.6
  38.6 0.0 copy-done.7
  38.6 0.2 fusion.21
  38.8 0.1 lt.61
  39.0 0.1 copy.33
  39.1 0.1 convert_reduce_fusion.2
  39.2 0.1 lt.64
  39.3 0.1 lt.65
  39.5 40.3 %all-to-all-done = bf16[128,4,768]{2,1,0:T(4,128)(2,1)S(1)} async-done(((bf16[128,4,768]{2,1,0:T(4,128)(2,1)}), bf16[128,4,768]{2,1,0:T(4,128)(2,1)S(1)}, u32[]{:S(2)}, u32[]{:S(2)}) %all-to-all-start) | async-done | bytes 786464 | tf_op jit(solution)/shard_map/all_to_all | solution.py:100
  79.8 0.1 copy.34
  79.9 0.8 copy.35
  80.7 0.0 copy-start.1
  80.7 0.3 reshape_reshape.12
  81.0 0.6 copy-done.1
  81.7 0.0 copy-start.2
  81.7 0.0 copy-start.3
  81.7 0.4 convolution_convert_fusion
  82.1 0.1 reshape_reshape.15
  82.2 0.5 copy-done.2
  82.7 0.4 convolution_convert_fusion.1
  83.1 0.0 copy-done.3
  83.1 0.4 convolution_convert_fusion.2
  83.5 0.1 reshape_reshape.13
  83.5 0.1 reshape_reshape.14
  83.6 0.7 fusion.33
  84.3 0.0 copy-start.4
  84.3 1.0 convert_reduce_fusion.1
  85.3 0.1 reduce_sum.71
  85.4 0.0 copy-done.4
  85.4 1.1 convolution_bitcast_fusion
  86.4 0.0 reduce-scatter.4.cloned.1.call-update
  86.5 20.8 %reduce-scatter.4.cloned.1.call-done = f32[192,2]{1,0:T(8,128)} async-done(((f32[768,2]{1,0:T(8,128)}), f32[192,2]{1,0:T(8,128)}) %reduce-scatter.4.cloned.1.call-update) | async-done | bytes 1552
  107.3 1.5 %copy.42 = bf16[2,192]{1,0:T(2,128)(2,1)} copy(f32[2,192]{0,1:T(8,128)} %bitcast.27) | data formatting | bytes 2304
  (10 shorter events, 0.1 us)
Async XLA Ops:
  7.2 5.2 %copy-start = (bf16[768,768]{1,0:T(8,128)(2,1)S(1)}, bf16[768,768]{1,0:T(8,128)(2,1)}, u32[]{:S(2)}) copy-start(bf16[768,768]{1,0:T(8,128)(2,1)} %param.11) | copy-start | bytes 3538948
  17.7 20.8 %copy-start.5 = (s32[45056]{0:T(1024)S(1)}, s32[45056]{0:T(1024)}, u32[]{:S(2)}) copy-start(s32[45056]{0:T(1024)} %param.17) | copy-start | bytes 540676
  17.7 20.9 %copy-start.6 = (s32[256]{0:T(256)S(1)}, s32[256]{0:T(256)}, u32[]{:S(2)}) copy-start(s32[256]{0:T(256)} %param.18) | copy-start | bytes 3076
  17.7 20.9 %copy-start.7 = (s32[256]{0:T(256)S(1)}, s32[256]{0:T(256)}, u32[]{:S(2)}) copy-start(s32[256]{0:T(256)} %param.19) | copy-start | bytes 3076
  17.7 62.1 %all-to-all-start = ((bf16[128,4,768]{2,1,0:T(4,128)(2,1)}), bf16[128,4,768]{2,1,0:T(4,128)(2,1)S(1)}, u32[]{:S(2)}, u32[]{:S(2)}) async-start(bf16[128,4,768]{2,1,0:T(4,128)(2,1)} %broadcast_select_fusion), calls=%async_computation | async-start | bytes 1572864 | tf_op jit(solution)/shard_map/all_to_all | solution.py:100
  38.4 68.9 %reduce-scatter.4.cloned.1.call-start = ((), (), s32[]{:S(2)}) async-start(), calls=%async_computation.2 | async-start | bytes 491520
  80.7 1.0 copy-start.1
  81.7 1.0 copy-start.2
  81.7 1.4 %copy-start.3 = (bf16[768,192]{0,1:T(8,128)(2,1)S(1)}, bf16[768,192]{0,1:T(8,128)(2,1)}, u32[]{:S(2)}) copy-start(bf16[768,192]{0,1:T(8,128)(2,1)} %param.15) | copy-start | bytes 884740
  84.3 1.0 copy-start.4
Sparse Core Ops, SparseCore 0:
  86.6 20.6 reduce-scatter.3
where the time goes:
time: 117 us; the launch traced here: 116 us
  waiting for transfers between devices  61.2 us (52%)
  starting transfers between devices  20.7 us (18%)
  between operations  14.3 us (12%)
  local copies, waits for them, and re-layouts  10.9 us (9%)
  matrix products  5.76 us (5%)
  other arithmetic  2.85 us (2%)
    all_to_all x1, waiting for transfers between devices, local(): lax.all_to_all(taken.reshape(shards, REG_DEV * per_shard, embedded.shape[...  40.3 us
    unnamed x2, waiting for transfers between devices  20.8 us
    all_to_all x1, starting transfers between devices, local(): lax.all_to_all(taken.reshape(shards, REG_DEV * per_shard, embedded.shape[...  20.7 us
    scatter x1, local copies, waits for them, and re-layouts, local(): jnp.full((slot_total,), -1, jnp.int32).at[flat]  2.91 us
    unnamed x17, local copies, waits for them, and re-layouts  2.71 us
  transfers between devices with their start and end apart: 2, of which 2 were waited for; matrix products, arithmetic and copies ran while one was open for 1% of the time, Pallas kernels for 0%

commit v1 on v0

v1 whole, which is shorter than its diff:
```python
import functools

import jax
import jax.numpy as jnp
from jax import lax
from jax.experimental import pallas as pl
from jax.experimental.pallas import tpu as pltpu
from jax.sharding import PartitionSpec as P

D = 768
SLOTS = 256
HD = 64
COLS = 192
TILE = 352
PAD = 384
NZ, NG, NX = 16, 8, 4
EMPTY = -8.0
MESH = pl.DeviceIdType.MESH
F32 = jnp.float32
BF16 = jnp.bfloat16
LAST = (((1,), (1,)), ((), ()))
GROUPS = ((0, 4), (4, 4), (8, 4), (12, 4))


def delta_of(p):
    if p == 0:
        return 0
    k = 8 - p // 2
    return k if p % 2 == 0 else 16 - k


def iota(shape, dim):
    return lax.broadcasted_iota(jnp.int32, shape, dim)


def kernel(
    feat, w, bias, wq, wk, wv, wo, reg, blk, cnt,
    mixed_out, region_out,
    f_v, w_v, bias_v, wq_v, wk_v, wv_v, wo_v, reg_v, blk_v, cnt_v,
    e_v, g_v, z_v, a_v, q_v, k_v, o_v, s_v, r_v,
    in_sem, own_sem, gs_sem, gr_sem, zs_sem, zr_sem, xs_sem, xr_sem, ps_sem, pr_sem, out_sem,
):
    dp = lax.axis_index("dp")
    h = lax.axis_index("head")
    z = dp // NG
    g = dp % NG

    first_row = (dp * TILE) // 128
    lane_off = (dp * TILE) % 128
    reg_base = pl.multiple_of(jnp.minimum((first_row // 8) * 8, TILE - 16), 8)
    loads = [
        pltpu.make_async_copy(reg.at[pl.ds(reg_base, 16)], reg_v, in_sem.at[0]),
        pltpu.make_async_copy(blk, blk_v, in_sem.at[1]),
        pltpu.make_async_copy(feat, f_v.at[pl.ds(0, TILE)], in_sem.at[2]),
        pltpu.make_async_copy(w, w_v, in_sem.at[3]),
        pltpu.make_async_copy(bias, bias_v, in_sem.at[4]),
        pltpu.make_async_copy(wq, wq_v, in_sem.at[5]),
        pltpu.make_async_copy(wk, wk_v, in_sem.at[6]),
        pltpu.make_async_copy(wv, wv_v, in_sem.at[7]),
        pltpu.make_async_copy(wo, wo_v, in_sem.at[8]),
        pltpu.make_async_copy(cnt, cnt_v, in_sem.at[9]),
    ]
    for load in loads:
        load.start()

    barrier = pltpu.get_barrier_semaphore()
    for o in range(1, NG):
        pl.semaphore_signal(
            barrier, inc=1, device_id={"dp": z * NG + (g + o) % NG, "head": h}, device_id_type=MESH
        )
    for o in range(1, NZ):
        pl.semaphore_signal(
            barrier, inc=1, device_id={"dp": ((z + o) % NZ) * NG + g, "head": h}, device_id_type=MESH
        )
    for o in range(1, NX):
        pl.semaphore_signal(
            barrier, inc=1, device_id={"dp": dp, "head": (h + o) % NX}, device_id_type=MESH
        )

    f_v[pl.ds(TILE, PAD - TILE), :] = jnp.zeros((PAD - TILE, D), BF16)
    upper = (iota((PAD, PAD), 0) < iota((PAD, PAD), 1)).astype(F32).astype(BF16)
    loads[0].wait()
    loads[1].wait()
    parts = []
    for i in range(4):
        at = jnp.minimum(first_row + i, TILE - 1) - reg_base
        parts.append(reg_v[pl.ds(at, 1), :])
    line = jnp.broadcast_to(jnp.concatenate(parts, axis=1), (8, 512))
    line = pltpu.roll(line, (512 - lane_off) % 512, 1)[:, :PAD]
    in_range = iota((8, PAD), 1) < TILE
    line = jnp.where(in_range, line, -1)
    hot = (iota((256, PAD), 0) == line[0:1, :]).astype(F32)
    hot16 = hot.astype(BF16)
    block_row = jnp.broadcast_to(blk_v[...].astype(F32), (8, 256)).astype(BF16)
    block = jnp.dot(block_row, hot16, preferred_element_type=F32)
    before = jnp.dot(hot16, upper, preferred_element_type=F32)
    rank = jnp.sum(before * hot, axis=0, keepdims=True)
    code = jnp.where(in_range[0:1, :], block[0:1, :] * 2.0 + rank, -1.0)
    row = iota((128, PAD), 0)
    target = (4 * ((row % NZ) * NG + row // NZ) + h).astype(F32)
    pick = (code == target).astype(F32)
    live = jnp.sum(pick, axis=1, keepdims=True)
    loads[2].wait()
    x = jnp.dot(pick.astype(BF16), f_v[...], preferred_element_type=F32).astype(BF16)
    loads[3].wait()
    loads[4].wait()
    hidden = jnp.dot(x, w_v[...], preferred_element_type=F32) + bias_v[...]
    embedded = jax.nn.gelu(hidden, approximate=True)
    embedded = jnp.where(live > 0.5, embedded, EMPTY).astype(BF16)
    e_v[...] = embedded.reshape(NG, NZ, D)

    pl.semaphore_wait(barrier, NG + NZ + NX - 3)

    g_sends = []
    for o in range(1, NG):
        to = (g + o) % NG
        copy = pltpu.make_async_remote_copy(
            src_ref=e_v.at[to],
            dst_ref=g_v.at[g],
            send_sem=gs_sem.at[o - 1],
            recv_sem=gr_sem.at[o - 1],
            device_id={"dp": z * NG + to, "head": h},
            device_id_type=MESH,
        )
        copy.start()
        g_sends.append(copy)
    g_v[pl.ds(g, 1)] = e_v[pl.ds(g, 1)]
    order = (iota((128, 128), 1) == (iota((128, 128), 0) % NG) * NZ + iota((128, 128), 0) // NG)
    order = order.astype(F32).astype(BF16)
    for copy in g_sends:
        copy.wait_recv()
    by_z = jnp.dot(order, g_v[...].reshape(128, D), preferred_element_type=F32).astype(BF16)
    z_v[...] = by_z.reshape(NZ, NG, D)

    z_sends = {}
    for p in range(1, NZ):
        to = (z + NZ - delta_of(p)) % NZ
        copy = pltpu.make_async_remote_copy(
            src_ref=z_v.at[to],
            dst_ref=a_v.at[h, p],
            send_sem=zs_sem.at[p],
            recv_sem=zr_sem.at[p],
            device_id={"dp": to * NG + g, "head": h},
            device_id_type=MESH,
        )
        copy.start()
        z_sends[p] = copy
    own = pltpu.make_async_copy(z_v.at[z], a_v.at[h, 0], own_sem)
    own.start()

    x_sends = []
    for n, (start, size) in enumerate(GROUPS):
        for p in range(start, start + size):
            if p == 0:
                own.wait()
            else:
                z_sends[p].wait_recv()
        sends = []
        for o in range(1, NX):
            copy = pltpu.make_async_remote_copy(
                src_ref=a_v.at[h, pl.ds(start, size)],
                dst_ref=a_v.at[h, pl.ds(start, size)],
                send_sem=xs_sem.at[n, o - 1],
                recv_sem=xr_sem.at[n, o - 1],
                device_id={"dp": dp, "head": (h + o) % NX},
                device_id_type=MESH,
            )
            copy.start()
            sends.append(copy)
        x_sends.append(sends)

    loads[5].wait()
    loads[6].wait()
    for n, (start, size) in enumerate(GROUPS):
        for copy in x_sends[n]:
            copy.wait_recv()
        rows = a_v[:, pl.ds(start, size)].reshape(NX * size * NG, D)
        place = pl.ds(start * NG, size * NG)
        for weight, kept in ((wq_v, q_v), (wk_v, k_v)):
            made = lax.dot_general(rows, weight[...], LAST, preferred_element_type=F32)
            kept[:, place] = made.astype(BF16).reshape(NX, size * NG, COLS)

    lane = iota((SLOTS, COLS), 1)
    at = iota((SLOTS, SLOTS), 0)
    slot = iota((SLOTS, SLOTS), 1)
    place = (at % 128) // NG
    k_off = 8 - place // 2
    off = jnp.where(place % 2 == 0, k_off, NZ - k_off)
    off = jnp.where(place == 0, 0, off)
    to_slot = (((z + off) % NZ) * NG + at % NG) * 2 + at // 128
    perm = (slot == to_slot).astype(F32)
    ones = jnp.ones((8, SLOTS), BF16)
    loads[7].wait()
    sums = []
    outs = []
    for j in range(2):
        queries = q_v[2 * j : 2 * j + 2].reshape(SLOTS, COLS)
        keys = k_v[2 * j : 2 * j + 2].reshape(SLOTS, COLS)
        rows = a_v[2 * j : 2 * j + 2].reshape(SLOTS, D)
        vals = lax.dot_general(wv_v[...], rows, LAST, preferred_element_type=F32).astype(BF16)
        alive = rows[:, 0:1].astype(F32) > -4.0
        shut = jnp.where(alive, 0.0, -1e30)
        parts = []
        for n in range(3):
            mine = (lane >= n * HD) & (lane < (n + 1) * HD)
            head_keys = jnp.where(mine, keys, jnp.zeros_like(keys))
            scores = lax.dot_general(head_keys, queries, LAST, preferred_element_type=F32)
            scores = scores * (HD ** -0.5) + shut
            top = jnp.max(scores, axis=0, keepdims=True)
            weights = jnp.exp(scores - top)
            inverse = 1.0 / jnp.sum(weights, axis=0, keepdims=True)
            part = jnp.dot(
                vals[n * HD : (n + 1) * HD], weights.astype(BF16), preferred_element_type=F32
            )
            parts.append((part * inverse).astype(BF16))
        mixed = jnp.concatenate(parts, axis=0)
        ordered = jnp.where(alive, perm, 0.0).astype(BF16)
        result = jnp.dot(mixed, ordered, preferred_element_type=F32).astype(BF16)
        o_v[j] = result
        out = pltpu.make_async_copy(o_v.at[j], mixed_out.at[j], out_sem.at[j])
        out.start()
        outs.append(out)
        sums.append(lax.dot_general(ones, result, LAST, preferred_element_type=F32)[0:1])

    loads[8].wait()
    loads[9].wait()
    pooled = []
    for j in range(2):
        here = blk_v[...] == dp * 2 + j
        count = jnp.sum(jnp.where(here, cnt_v[...].astype(F32), 0.0), axis=1, keepdims=True)
        pooled.append(sums[j] / count)
    pooled = jnp.concatenate(pooled + [jnp.zeros((6, COLS), F32)], axis=0).astype(BF16)
    partial = jnp.dot(pooled, wo_v[...], preferred_element_type=F32)
    for i in range(NX):
        s_v[i, :, 0:COLS] = partial[:, i * COLS : (i + 1) * COLS]
        s_v[i, :, COLS:256] = jnp.zeros((8, 256 - COLS), F32)
    p_sends = []
    for o in range(1, NX):
        to = (h + o) % NX
        copy = pltpu.make_async_remote_copy(
            src_ref=s_v.at[to],
            dst_ref=r_v.at[o - 1],
            send_sem=ps_sem.at[o - 1],
            recv_sem=pr_sem.at[o - 1],
            device_id={"dp": dp, "head": to},
            device_id_type=MESH,
        )
        copy.start()
        p_sends.append(copy)
    for copy in g_sends:
        copy.wait_send()
    for copy in z_sends.values():
        copy.wait_send()
    for sends in x_sends:
        for copy in sends:
            copy.wait_send()
    own_part = s_v[h]
    for copy in p_sends:
        copy.wait_recv()
    everything = own_part + r_v[0] + r_v[1] + r_v[2]
    region_out[...] = everything[0:2, 0:COLS].astype(BF16)
    for copy in p_sends:
        copy.wait_send()
    for out in outs:
        out.wait()


def local(
    tile_features, tile_weight, tile_bias, query_weight, key_weight, value_weight, output_weight,
    tile_region, region_block, region_count,
):
    dma = pltpu.SemaphoreType.DMA
    anywhere = pl.BlockSpec(memory_space=pl.ANY)
    groups = len(GROUPS)
    mixed, region = pl.pallas_call(
        kernel,
        out_shape=(
            jax.ShapeDtypeStruct((2, COLS, SLOTS), BF16),
            jax.ShapeDtypeStruct((2, COLS), BF16),
        ),
        in_specs=[anywhere] * 10,
        out_specs=(anywhere, pl.BlockSpec(memory_space=pltpu.VMEM)),
        scratch_shapes=[
            pltpu.VMEM((PAD, D), BF16),
            pltpu.VMEM((D, D), BF16),
            pltpu.VMEM((1, D), F32),
            pltpu.VMEM((COLS, D), BF16),
            pltpu.VMEM((COLS, D), BF16),
            pltpu.VMEM((COLS, D), BF16),
            pltpu.VMEM((COLS, D), BF16),
            pltpu.VMEM((16, 128), jnp.int32),
            pltpu.VMEM((1, 256), jnp.int32),
            pltpu.VMEM((1, 256), jnp.int32),
            pltpu.VMEM((NG, NZ, D), BF16),
            pltpu.VMEM((NG, NZ, D), BF16),
            pltpu.VMEM((NZ, NG, D), BF16),
            pltpu.VMEM((NX, NZ, NG, D), BF16),
            pltpu.VMEM((NX, 128, COLS), BF16),
            pltpu.VMEM((NX, 128, COLS), BF16),
            pltpu.VMEM((2, COLS, SLOTS), BF16),
            pltpu.VMEM((NX, 8, 256), F32),
            pltpu.VMEM((NX - 1, 8, 256), F32),
            dma((10,)),
            dma,
            dma((NG - 1,)),
            dma((NG - 1,)),
            dma((NZ,)),
            dma((NZ,)),
            dma((groups, NX - 1)),
            dma((groups, NX - 1)),
            dma((NX - 1,)),
            dma((NX - 1,)),
            dma((2,)),
        ],
        compiler_params=pltpu.CompilerParams(
            collective_id=0, has_side_effects=True, vmem_limit_bytes=60 * 1024 * 1024
        ),
        name="regroup_attend",
    )(
        tile_features, tile_weight, tile_bias.reshape(1, D), query_weight.T, key_weight.T, value_weight.T,
        output_weight, tile_region.reshape(TILE, 128), region_block.reshape(1, 256),
        region_count.reshape(1, 256),
    )
    return mixed.transpose(0, 2, 1), region


def solution(mesh):
    in_specs = (
        P("dp", None),
        P(),
        P(),
        P(None, "head"),
        P(None, "head"),
        P(None, "head"),
        P("head", None),
        P(),
        P(),
        P(),
    )
    out_specs = (P("dp", None, "head"), P("dp", "head"))
    return jax.shard_map(local, mesh=mesh, in_specs=in_specs, out_specs=out_specs, check_vma=False)
```

time: 117 us -> 52 us (0.44)
  the two profiles are of different devices: /device:TPU:1 before, /device:TPU:4 now
where the time goes in v1:
time: 52 us; the launch traced here: 51.8 us
  Pallas kernels  47.1 us (91%)
  local copies, waits for them, and re-layouts  4.07 us (8%)
  between operations  0.64 us (1%)
    pallas_call x1, Pallas kernels, local(): pl.pallas_call(kernel, out_shape=(jax.ShapeDtypeStruct((2, COLS, SLOTS),...  47.1 us
    unnamed x2, local copies, waits for them, and re-layouts  2.8 us
    reshape x1, local copies, waits for them, and re-layouts, local(): tile_bias.reshape(1, D)  1.27 us

profile of v1, /device:TPU:4, one launch (start us, length us, event | category | flops | bytes accessed | tf_op | source)
XLA Modules:
  0.0 51.8 jit_solution(15866859653606320315)
XLA Ops:
  0.6 1.3 %reshape.16.bias = f32[1,768]{1,0:T(1,128)} reshape(f32[768]{0:T(1024)} %param.12) | data formatting | bytes 6144 | tf_op jit(solution)/shard_map/reshape | solution.py:320
  1.9 47.1 %regroup_attend.1 = (bf16[2,192,256]{2,1,0:T(8,128)(2,1)}, bf16[2,192]{1,0:T(2,128)(2,1)}) custom-call(bf16[352,768]{1,0:T(8,128)(2,1)} %feat.1, bf16[768,768]{1,0:T(8,128)(2,1)} %w.1, f32[1,768]{1,0:T(1,128)} %reshape.16.bias, bf16[192,768]{1,0:T(8,128)(2,1)} %bitcast.7, bf16[192,768]{1,0:T(8,128)(2,1)} %bitcast.8, bf16[192,768]{1,0:T(8,128)(2,1)} %bitcast.9, ...), custom_call_target="tpu_custom_call" | custom-call | tf_op jit(solution)/shard_map/regroup_attend/pallas_call | solution.py:275
  49.0 1.6 %copy.14 = bf16[2,256,192]{1,2,0:T(8,128)(2,1)} copy(bf16[2,256,192]{1,2,0:T(8,128)(2,1)} %bitcast.10) | data formatting | bytes 393216
  50.6 1.2 %copy.15 = bf16[2,192]{1,0:T(2,128)(2,1)} copy(bf16[2,192]{1,0:T(2,128)(2,1)} %get-tuple-element.9) | data formatting | bytes 1536

commit v2 on v1

--- a/solution.py
+++ b/solution.py
@@ -19,14 +19,9 @@
 F32 = jnp.float32
 BF16 = jnp.bfloat16
 LAST = (((1,), (1,)), ((), ()))
-GROUPS = ((0, 4), (4, 4), (8, 4), (12, 4))
-
-
-def delta_of(p):
-    if p == 0:
-        return 0
-    k = 8 - p // 2
-    return k if p % 2 == 0 else 16 - k
+CHUNK = 4
+CHUNKS = NZ // CHUNK
+OFFSETS = (0, 1, 15, 2, 14, 3, 13, 4, 12, 5, 11, 6, 10, 7, 9, 8)
 
 
 def iota(shape, dim):
@@ -37,13 +32,15 @@
     feat, w, bias, wq, wk, wv, wo, reg, blk, cnt,
     mixed_out, region_out,
     f_v, w_v, bias_v, wq_v, wk_v, wv_v, wo_v, reg_v, blk_v, cnt_v,
-    e_v, g_v, z_v, a_v, q_v, k_v, o_v, s_v, r_v,
-    in_sem, own_sem, gs_sem, gr_sem, zs_sem, zr_sem, xs_sem, xr_sem, ps_sem, pr_sem, out_sem,
+    e_v, z_v, c_v, a_v, perm_v, o_v, s_v, r_v,
+    in_sem, own_sem, zs_sem, zr_sem, xs_sem, xr_sem, ps_sem, pr_sem, out_sem,
 ):
     dp = lax.axis_index("dp")
     h = lax.axis_index("head")
     z = dp // NG
     g = dp % NG
+    y = g // 2
+    core = g % 2
 
     first_row = (dp * TILE) // 128
     lane_off = (dp * TILE) % 128
@@ -64,10 +61,18 @@
         load.start()
 
     barrier = pltpu.get_barrier_semaphore()
-    for o in range(1, NG):
-        pl.semaphore_signal(
-            barrier, inc=1, device_id={"dp": z * NG + (g + o) % NG, "head": h}, device_id_type=MESH
-        )
+    for o in range(NG):
+        source = (g + o) % NG
+        if o == 0:
+            @pl.when(y != h)
+            def _():
+                pl.semaphore_signal(
+                    barrier, inc=1, device_id={"dp": dp, "head": y}, device_id_type=MESH
+                )
+        else:
+            pl.semaphore_signal(
+                barrier, inc=1, device_id={"dp": z * NG + source, "head": y}, device_id_type=MESH
+            )
     for o in range(1, NZ):
         pl.semaphore_signal(
             barrier, inc=1, device_id={"dp": ((z + o) % NZ) * NG + g, "head": h}, device_id_type=MESH
@@ -97,47 +102,26 @@
     rank = jnp.sum(before * hot, axis=0, keepdims=True)
     code = jnp.where(in_range[0:1, :], block[0:1, :] * 2.0 + rank, -1.0)
     row = iota((128, PAD), 0)
-    target = (4 * ((row % NZ) * NG + row // NZ) + h).astype(F32)
+    target = (32 * (row // NG) + 8 * h + row % NG).astype(F32)
     pick = (code == target).astype(F32)
     live = jnp.sum(pick, axis=1, keepdims=True)
     loads[2].wait()
     x = jnp.dot(pick.astype(BF16), f_v[...], preferred_element_type=F32).astype(BF16)
     loads[3].wait()
     loads[4].wait()
-    hidden = jnp.dot(x, w_v[...], preferred_element_type=F32) + bias_v[...]
+    hidden = jnp.dot(x, w_v[...], preferred_element_type=F32) + bias_v[...].reshape(1, D)
     embedded = jax.nn.gelu(hidden, approximate=True)
     embedded = jnp.where(live > 0.5, embedded, EMPTY).astype(BF16)
-    e_v[...] = embedded.reshape(NG, NZ, D)
-
-    pl.semaphore_wait(barrier, NG + NZ + NX - 3)
-
-    g_sends = []
-    for o in range(1, NG):
-        to = (g + o) % NG
+    e_v[...] = embedded.reshape(NZ, NG, D)
+
+    pl.semaphore_wait(barrier, NG + NZ - 1 + NX - 1 - (y == h).astype(jnp.int32))
+
+    z_sends = {}
+    for p in range(1, NZ):
+        to = (z + NZ - OFFSETS[p]) % NZ
         copy = pltpu.make_async_remote_copy(
             src_ref=e_v.at[to],
-            dst_ref=g_v.at[g],
-            send_sem=gs_sem.at[o - 1],
-            recv_sem=gr_sem.at[o - 1],
-            device_id={"dp": z * NG + to, "head": h},
-            device_id_type=MESH,
-        )
-        copy.start()
-        g_sends.append(copy)
-    g_v[pl.ds(g, 1)] = e_v[pl.ds(g, 1)]
-    order = (iota((128, 128), 1) == (iota((128, 128), 0) % NG) * NZ + iota((128, 128), 0) // NG)
-    order = order.astype(F32).astype(BF16)
-    for copy in g_sends:
-        copy.wait_recv()
-    by_z = jnp.dot(order, g_v[...].reshape(128, D), preferred_element_type=F32).astype(BF16)
-    z_v[...] = by_z.reshape(NZ, NG, D)
-
-    z_sends = {}
-    for p in range(1, NZ):
-        to = (z + NZ - delta_of(p)) % NZ
-        copy = pltpu.make_async_remote_copy(
-            src_ref=z_v.at[to],
-            dst_ref=a_v.at[h, p],
+            dst_ref=z_v.at[p],
             send_sem=zs_sem.at[p],
             recv_sem=zr_sem.at[p],
             device_id={"dp": to * NG + g, "head": h},
@@ -145,58 +129,72 @@
         )
         copy.start()
         z_sends[p] = copy
-    own = pltpu.make_async_copy(z_v.at[z], a_v.at[h, 0], own_sem)
+    own = pltpu.make_async_copy(e_v.at[z], z_v.at[0], own_sem)
     own.start()
 
+    at = iota((SLOTS, SLOTS), 0)
+    slot = iota((SLOTS, SLOTS), 1)
+    place = (at // 8 % CHUNKS) * CHUNK + at % CHUNK
+    off = jnp.zeros((SLOTS, SLOTS), jnp.int32)
+    for p in range(1, NZ):
+        off = jnp.where(place == p, OFFSETS[p], off)
+    to_slot = (((z + off) % NZ) * NG + at // 32) * 2 + at // CHUNK % 2
+    perm_v[...] = (slot == to_slot).astype(F32).astype(BF16)
+
+    rows = 8 * CHUNK
+    out_row = iota((rows, rows), 0)
+    in_row = (out_row % CHUNK) * 8 + out_row // 8 % 2 * 2 + out_row // 16 * 4 + out_row // CHUNK % 2
+    order = (iota((rows, rows), 1) == in_row).astype(F32).astype(BF16)
     x_sends = []
-    for n, (start, size) in enumerate(GROUPS):
-        for p in range(start, start + size):
+    local_sends = []
+    for n in range(CHUNKS):
+        for p in range(n * CHUNK, (n + 1) * CHUNK):
             if p == 0:
                 own.wait()
             else:
                 z_sends[p].wait_recv()
-        sends = []
-        for o in range(1, NX):
-            copy = pltpu.make_async_remote_copy(
-                src_ref=a_v.at[h, pl.ds(start, size)],
-                dst_ref=a_v.at[h, pl.ds(start, size)],
-                send_sem=xs_sem.at[n, o - 1],
-                recv_sem=xr_sem.at[n, o - 1],
-                device_id={"dp": dp, "head": (h + o) % NX},
-                device_id_type=MESH,
-            )
-            copy.start()
-            sends.append(copy)
-        x_sends.append(sends)
+        arrived = z_v[n * CHUNK : (n + 1) * CHUNK].reshape(rows, D)
+        turned = jnp.dot(order, arrived, preferred_element_type=F32).astype(BF16)
+        c_v[n] = turned.reshape(2, 2, 2 * CHUNK, D)
+        for o in (2, 1, 3, 0):
+            for oc in (1, 0):
+                to = (h + o) % NX
+                to_core = (core + oc) % 2
+                copy = pltpu.make_async_remote_copy(
+                    src_ref=c_v.at[n, to_core],
+                    dst_ref=a_v.at[:, g, n],
+                    send_sem=xs_sem.at[n, o, oc],
+                    recv_sem=xr_sem.at[n, g],
+                    device_id={"dp": z * NG + h * 2 + to_core, "head": to},
+                    device_id_type=MESH,
+                )
+                if o == 0 and oc == 0:
+                    here = pltpu.make_async_copy(
+                        c_v.at[n, to_core], a_v.at[:, g, n], xr_sem.at[n, g]
+                    )
+                    pl.when(y == h)(here.start)
+                    pl.when(y != h)(copy.start)
+                    local_sends.append(copy)
+                else:
+                    copy.start()
+                    x_sends.append(copy)
 
     loads[5].wait()
     loads[6].wait()
-    for n, (start, size) in enumerate(GROUPS):
-        for copy in x_sends[n]:
-            copy.wait_recv()
-        rows = a_v[:, pl.ds(start, size)].reshape(NX * size * NG, D)
-        place = pl.ds(start * NG, size * NG)
-        for weight, kept in ((wq_v, q_v), (wk_v, k_v)):
-            made = lax.dot_general(rows, weight[...], LAST, preferred_element_type=F32)
-            kept[:, place] = made.astype(BF16).reshape(NX, size * NG, COLS)
+    loads[7].wait()
+    for n in range(CHUNKS):
+        for source in range(NG):
+            landed = a_v.at[:, source, n]
+            pltpu.make_async_copy(landed, landed, xr_sem.at[n, source]).wait()
 
     lane = iota((SLOTS, COLS), 1)
-    at = iota((SLOTS, SLOTS), 0)
-    slot = iota((SLOTS, SLOTS), 1)
-    place = (at % 128) // NG
-    k_off = 8 - place // 2
-    off = jnp.where(place % 2 == 0, k_off, NZ - k_off)
-    off = jnp.where(place == 0, 0, off)
-    to_slot = (((z + off) % NZ) * NG + at % NG) * 2 + at // 128
-    perm = (slot == to_slot).astype(F32)
     ones = jnp.ones((8, SLOTS), BF16)
-    loads[7].wait()
     sums = []
     outs = []
     for j in range(2):
-        queries = q_v[2 * j : 2 * j + 2].reshape(SLOTS, COLS)
-        keys = k_v[2 * j : 2 * j + 2].reshape(SLOTS, COLS)
-        rows = a_v[2 * j : 2 * j + 2].reshape(SLOTS, D)
+        rows = a_v[j].reshape(SLOTS, D)
+        queries = lax.dot_general(rows, wq_v[...], LAST, preferred_element_type=F32).astype(BF16)
+        keys = lax.dot_general(rows, wk_v[...], LAST, preferred_element_type=F32).astype(BF16)
         vals = lax.dot_general(wv_v[...], rows, LAST, preferred_element_type=F32).astype(BF16)
         alive = rows[:, 0:1].astype(F32) > -4.0
         shut = jnp.where(alive, 0.0, -1e30)
@@ -214,7 +212,7 @@
             )
             parts.append((part * inverse).astype(BF16))
         mixed = jnp.concatenate(parts, axis=0)
-        ordered = jnp.where(alive, perm, 0.0).astype(BF16)
+        ordered = jnp.where(alive, perm_v[...].astype(F32), 0.0).astype(BF16)
         result = jnp.dot(mixed, ordered, preferred_element_type=F32).astype(BF16)
         o_v[j] = result
         out = pltpu.make_async_copy(o_v.at[j], mixed_out.at[j], out_sem.at[j])
@@ -247,13 +245,12 @@
         )
         copy.start()
         p_sends.append(copy)
-    for copy in g_sends:
-        copy.wait_send()
     for copy in z_sends.values():
         copy.wait_send()
-    for sends in x_sends:
-        for copy in sends:
-            copy.wait_send()
+    for copy in x_sends:
+        copy.wait_send()
+    for copy in local_sends:
+        pl.when(y != h)(copy.wait_send)
     own_part = s_v[h]
     for copy in p_sends:
         copy.wait_recv()
@@ -271,7 +268,6 @@
 ):
     dma = pltpu.SemaphoreType.DMA
     anywhere = pl.BlockSpec(memory_space=pl.ANY)
-    groups = len(GROUPS)
     mixed, region = pl.pallas_call(
         kernel,
         out_shape=(
@@ -283,7 +279,7 @@
         scratch_shapes=[
             pltpu.VMEM((PAD, D), BF16),
             pltpu.VMEM((D, D), BF16),
-            pltpu.VMEM((1, D), F32),
+            pltpu.VMEM((D,), F32),
             pltpu.VMEM((COLS, D), BF16),
             pltpu.VMEM((COLS, D), BF16),
             pltpu.VMEM((COLS, D), BF16),
@@ -291,23 +287,20 @@
             pltpu.VMEM((16, 128), jnp.int32),
             pltpu.VMEM((1, 256), jnp.int32),
             pltpu.VMEM((1, 256), jnp.int32),
-            pltpu.VMEM((NG, NZ, D), BF16),
-            pltpu.VMEM((NG, NZ, D), BF16),
             pltpu.VMEM((NZ, NG, D), BF16),
-            pltpu.VMEM((NX, NZ, NG, D), BF16),
-            pltpu.VMEM((NX, 128, COLS), BF16),
-            pltpu.VMEM((NX, 128, COLS), BF16),
+            pltpu.VMEM((NZ, NG, D), BF16),
+            pltpu.VMEM((CHUNKS, 2, 2, 2 * CHUNK, D), BF16),
+            pltpu.VMEM((2, NG, CHUNKS, 2 * CHUNK, D), BF16),
+            pltpu.VMEM((SLOTS, SLOTS), BF16),
             pltpu.VMEM((2, COLS, SLOTS), BF16),
             pltpu.VMEM((NX, 8, 256), F32),
             pltpu.VMEM((NX - 1, 8, 256), F32),
             dma((10,)),
             dma,
-            dma((NG - 1,)),
-            dma((NG - 1,)),
             dma((NZ,)),
             dma((NZ,)),
-            dma((groups, NX - 1)),
-            dma((groups, NX - 1)),
+            dma((CHUNKS, NX, 2)),
+            dma((CHUNKS, NG)),
             dma((NX - 1,)),
             dma((NX - 1,)),
             dma((2,)),
@@ -317,7 +310,7 @@
         ),
         name="regroup_attend",
     )(
-        tile_features, tile_weight, tile_bias.reshape(1, D), query_weight.T, key_weight.T, value_weight.T,
+        tile_features, tile_weight, tile_bias, query_weight.T, key_weight.T, value_weight.T,
         output_weight, tile_region.reshape(TILE, 128), region_block.reshape(1, 256),
         region_count.reshape(1, 256),
     )

time: 52 us -> 44.8 us (0.86)
  the two profiles are of different devices: /device:TPU:4 before, /device:TPU:1 now
where the time goes in v2:
time: 44.8 us; the launch traced here: 44.4 us
  Pallas kernels  41 us (92%)
  local copies, waits for them, and re-layouts  2.8 us (6%)
  between operations  0.64 us (1%)
    pallas_call x1, Pallas kernels, local(): pl.pallas_call(kernel, out_shape=(jax.ShapeDtypeStruct((2, COLS, SLOTS),...  41 us
    unnamed x2, local copies, waits for them, and re-layouts  2.8 us

profile of v2, /device:TPU:1, one launch (start us, length us, event | category | flops | bytes accessed | tf_op | source)
XLA Modules:
  0.0 44.4 jit_solution(4082462410144716305)
XLA Ops:
  0.6 41.0 %regroup_attend.1 = (bf16[2,192,256]{2,1,0:T(8,128)(2,1)}, bf16[2,192]{1,0:T(2,128)(2,1)}) custom-call(bf16[352,768]{1,0:T(8,128)(2,1)} %feat.1, bf16[768,768]{1,0:T(8,128)(2,1)} %w.1, f32[768]{0:T(1024)} %bias.1, bf16[192,768]{1,0:T(8,128)(2,1)} %bitcast.7, bf16[192,768]{1,0:T(8,128)(2,1)} %bitcast.8, bf16[192,768]{1,0:T(8,128)(2,1)} %bitcast.9, ...), custom_call_target="tpu_custom_call" | custom-call | tf_op jit(solution)/shard_map/regroup_attend/pallas_call | solution.py:271
  41.6 1.6 %copy.14 = bf16[2,256,192]{1,2,0:T(8,128)(2,1)} copy(bf16[2,256,192]{1,2,0:T(8,128)(2,1)} %bitcast.10) | data formatting | bytes 393216
  43.3 1.2 %copy.15 = bf16[2,192]{1,0:T(2,128)(2,1)} copy(bf16[2,192]{1,0:T(2,128)(2,1)} %get-tuple-element.9) | data formatting | bytes 1536

commit v3 on v2

--- a/solution.py
+++ b/solution.py
@@ -22,6 +22,7 @@
 CHUNK = 4
 CHUNKS = NZ // CHUNK
 OFFSETS = (0, 1, 15, 2, 14, 3, 13, 4, 12, 5, 11, 6, 10, 7, 9, 8)
+ISSUE = (1, 15, 2, 14, 3, 13, 4, 12, 5, 11, 6, 10, 7, 9, 8)
 
 
 def iota(shape, dim):
@@ -32,8 +33,8 @@
     feat, w, bias, wq, wk, wv, wo, reg, blk, cnt,
     mixed_out, region_out,
     f_v, w_v, bias_v, wq_v, wk_v, wv_v, wo_v, reg_v, blk_v, cnt_v,
-    e_v, z_v, c_v, a_v, perm_v, o_v, s_v, r_v,
-    in_sem, own_sem, zs_sem, zr_sem, xs_sem, xr_sem, ps_sem, pr_sem, out_sem,
+    e_v, z_v, c_v, a_v, q_v, k_v, perm_v, s_v, r_v,
+    in_sem, own_sem, zs_sem, zr_sem, xs_sem, xr_sem, ps_sem, pr_sem,
 ):
     dp = lax.axis_index("dp")
     h = lax.axis_index("head")
@@ -117,8 +118,9 @@
     pl.semaphore_wait(barrier, NG + NZ - 1 + NX - 1 - (y == h).astype(jnp.int32))
 
     z_sends = {}
-    for p in range(1, NZ):
-        to = (z + NZ - OFFSETS[p]) % NZ
+    for offset in ISSUE:
+        p = OFFSETS.index(offset)
+        to = (z + NZ - offset) % NZ
         copy = pltpu.make_async_remote_copy(
             src_ref=e_v.at[to],
             dst_ref=z_v.at[p],
@@ -134,11 +136,11 @@
 
     at = iota((SLOTS, SLOTS), 0)
     slot = iota((SLOTS, SLOTS), 1)
-    place = (at // 8 % CHUNKS) * CHUNK + at % CHUNK
+    place = (at // 64) * CHUNK + at % CHUNK
     off = jnp.zeros((SLOTS, SLOTS), jnp.int32)
     for p in range(1, NZ):
         off = jnp.where(place == p, OFFSETS[p], off)
-    to_slot = (((z + off) % NZ) * NG + at // 32) * 2 + at // CHUNK % 2
+    to_slot = (((z + off) % NZ) * NG + at // 8 % NG) * 2 + at // CHUNK % 2
     perm_v[...] = (slot == to_slot).astype(F32).astype(BF16)
 
     rows = 8 * CHUNK
@@ -162,7 +164,7 @@
                 to_core = (core + oc) % 2
                 copy = pltpu.make_async_remote_copy(
                     src_ref=c_v.at[n, to_core],
-                    dst_ref=a_v.at[:, g, n],
+                    dst_ref=a_v.at[:, n, g],
                     send_sem=xs_sem.at[n, o, oc],
                     recv_sem=xr_sem.at[n, g],
                     device_id={"dp": z * NG + h * 2 + to_core, "head": to},
@@ -170,7 +172,7 @@
                 )
                 if o == 0 and oc == 0:
                     here = pltpu.make_async_copy(
-                        c_v.at[n, to_core], a_v.at[:, g, n], xr_sem.at[n, g]
+                        c_v.at[n, to_core], a_v.at[:, n, g], xr_sem.at[n, g]
                     )
                     pl.when(y == h)(here.start)
                     pl.when(y != h)(copy.start)
@@ -179,56 +181,58 @@
                     copy.start()
                     x_sends.append(copy)
 
-    loads[5].wait()
-    loads[6].wait()
-    loads[7].wait()
+    for load in loads[5:]:
+        load.wait()
+    counts = []
+    for j in range(2):
+        here = blk_v[...] == dp * 2 + j
+        counts.append(
+            jnp.sum(jnp.where(here, cnt_v[...].astype(F32), 0.0), axis=1, keepdims=True)
+        )
+    size = 16 * CHUNK
     for n in range(CHUNKS):
         for source in range(NG):
-            landed = a_v.at[:, source, n]
+            landed = a_v.at[:, n, source]
             pltpu.make_async_copy(landed, landed, xr_sem.at[n, source]).wait()
+        rows = a_v[:, n].reshape(2 * size, D)
+        for weight, kept in ((wk_v, k_v), (wq_v, q_v)):
+            made = lax.dot_general(rows, weight[...], LAST, preferred_element_type=F32)
+            kept[:, n * size : (n + 1) * size] = made.astype(BF16).reshape(2, size, COLS)
 
     lane = iota((SLOTS, COLS), 1)
-    ones = jnp.ones((8, SLOTS), BF16)
-    sums = []
-    outs = []
+    first = (iota((8, 128), 1) == 0).astype(F32).astype(BF16)
+    pairs = [(j, n) for j in range(2) for n in range(3)]
+    alive, alive_row, scores, vals = [], [], {}, []
+    for j in range(2):
+        marks = a_v[j, :, :, :, 0:128].reshape(SLOTS, 128)
+        alive.append(marks[:, 0:1].astype(F32) > -4.0)
+        mark = lax.dot_general(first, marks, LAST, preferred_element_type=F32)
+        alive_row.append((mark > -4.0).astype(F32).astype(BF16))
+    for j, n in pairs:
+        keys = k_v[j]
+        mine = (lane >= n * HD) & (lane < (n + 1) * HD)
+        head_keys = jnp.where(mine, keys, jnp.zeros_like(keys))
+        scores[j, n] = lax.dot_general(head_keys, q_v[j], LAST, preferred_element_type=F32)
     for j in range(2):
         rows = a_v[j].reshape(SLOTS, D)
-        queries = lax.dot_general(rows, wq_v[...], LAST, preferred_element_type=F32).astype(BF16)
-        keys = lax.dot_general(rows, wk_v[...], LAST, preferred_element_type=F32).astype(BF16)
-        vals = lax.dot_general(wv_v[...], rows, LAST, preferred_element_type=F32).astype(BF16)
-        alive = rows[:, 0:1].astype(F32) > -4.0
-        shut = jnp.where(alive, 0.0, -1e30)
-        parts = []
-        for n in range(3):
-            mine = (lane >= n * HD) & (lane < (n + 1) * HD)
-            head_keys = jnp.where(mine, keys, jnp.zeros_like(keys))
-            scores = lax.dot_general(head_keys, queries, LAST, preferred_element_type=F32)
-            scores = scores * (HD ** -0.5) + shut
-            top = jnp.max(scores, axis=0, keepdims=True)
-            weights = jnp.exp(scores - top)
-            inverse = 1.0 / jnp.sum(weights, axis=0, keepdims=True)
-            part = jnp.dot(
-                vals[n * HD : (n + 1) * HD], weights.astype(BF16), preferred_element_type=F32
-            )
-            parts.append((part * inverse).astype(BF16))
-        mixed = jnp.concatenate(parts, axis=0)
-        ordered = jnp.where(alive, perm_v[...].astype(F32), 0.0).astype(BF16)
-        result = jnp.dot(mixed, ordered, preferred_element_type=F32).astype(BF16)
-        o_v[j] = result
-        out = pltpu.make_async_copy(o_v.at[j], mixed_out.at[j], out_sem.at[j])
-        out.start()
-        outs.append(out)
-        sums.append(lax.dot_general(ones, result, LAST, preferred_element_type=F32)[0:1])
-
-    loads[8].wait()
-    loads[9].wait()
-    pooled = []
-    for j in range(2):
-        here = blk_v[...] == dp * 2 + j
-        count = jnp.sum(jnp.where(here, cnt_v[...].astype(F32), 0.0), axis=1, keepdims=True)
-        pooled.append(sums[j] / count)
-    pooled = jnp.concatenate(pooled + [jnp.zeros((6, COLS), F32)], axis=0).astype(BF16)
-    partial = jnp.dot(pooled, wo_v[...], preferred_element_type=F32)
+        made = lax.dot_general(wv_v[...], rows, LAST, preferred_element_type=F32)
+        vals.append(made.astype(BF16))
+    parts = {}
+    for j, n in pairs:
+        masked = scores[j, n] * (HD ** -0.5) + jnp.where(alive[j], 0.0, -1e30)
+        top = jnp.max(masked, axis=0, keepdims=True)
+        weights = jnp.exp(masked - top)
+        inverse = 1.0 / jnp.sum(weights, axis=0, keepdims=True)
+        part = jnp.dot(
+            vals[j][n * HD : (n + 1) * HD], weights.astype(BF16), preferred_element_type=F32
+        )
+        parts[j, n] = (part * inverse).astype(BF16)
+    mixed = [jnp.concatenate([parts[j, n] for n in range(3)], axis=0) for j in range(2)]
+    pooled = jnp.zeros((8, COLS), F32)
+    for j in range(2):
+        total = lax.dot_general(alive_row[j], mixed[j], LAST, preferred_element_type=F32)
+        pooled = jnp.where(iota((8, COLS), 0) == j, total / counts[j], pooled)
+    partial = jnp.dot(pooled.astype(BF16), wo_v[...], preferred_element_type=F32)
     for i in range(NX):
         s_v[i, :, 0:COLS] = partial[:, i * COLS : (i + 1) * COLS]
         s_v[i, :, COLS:256] = jnp.zeros((8, 256 - COLS), F32)
@@ -245,6 +249,10 @@
         )
         copy.start()
         p_sends.append(copy)
+    for j in range(2):
+        ordered = jnp.where(alive[j], perm_v[...].astype(F32), 0.0).astype(BF16)
+        result = jnp.dot(mixed[j], ordered, preferred_element_type=F32)
+        mixed_out[j] = result.astype(BF16)
     for copy in z_sends.values():
         copy.wait_send()
     for copy in x_sends:
@@ -258,8 +266,6 @@
     region_out[...] = everything[0:2, 0:COLS].astype(BF16)
     for copy in p_sends:
         copy.wait_send()
-    for out in outs:
-        out.wait()
 
 
 def local(
@@ -271,11 +277,11 @@
     mixed, region = pl.pallas_call(
         kernel,
         out_shape=(
-            jax.ShapeDtypeStruct((2, COLS, SLOTS), BF16),
-            jax.ShapeDtypeStruct((2, COLS), BF16),
+            pltpu.VMEM((2, COLS, SLOTS), BF16),
+            pltpu.VMEM((2, COLS), BF16),
         ),
         in_specs=[anywhere] * 10,
-        out_specs=(anywhere, pl.BlockSpec(memory_space=pltpu.VMEM)),
+        out_specs=(pl.BlockSpec(memory_space=pltpu.VMEM), pl.BlockSpec(memory_space=pltpu.VMEM)),
         scratch_shapes=[
             pltpu.VMEM((PAD, D), BF16),
             pltpu.VMEM((D, D), BF16),
@@ -290,9 +296,10 @@
             pltpu.VMEM((NZ, NG, D), BF16),
             pltpu.VMEM((NZ, NG, D), BF16),
             pltpu.VMEM((CHUNKS, 2, 2, 2 * CHUNK, D), BF16),
-            pltpu.VMEM((2, NG, CHUNKS, 2 * CHUNK, D), BF16),
+            pltpu.VMEM((2, CHUNKS, NG, 2 * CHUNK, D), BF16),
+            pltpu.VMEM((2, SLOTS, COLS), BF16),
+            pltpu.VMEM((2, SLOTS, COLS), BF16),
             pltpu.VMEM((SLOTS, SLOTS), BF16),
-            pltpu.VMEM((2, COLS, SLOTS), BF16),
             pltpu.VMEM((NX, 8, 256), F32),
             pltpu.VMEM((NX - 1, 8, 256), F32),
             dma((10,)),
@@ -303,7 +310,6 @@
             dma((CHUNKS, NG)),
             dma((NX - 1,)),
             dma((NX - 1,)),
-            dma((2,)),
         ],
         compiler_params=pltpu.CompilerParams(
             collective_id=0, has_side_effects=True, vmem_limit_bytes=60 * 1024 * 1024

time: 44.8 us -> 41.3 us (0.922)
  Pallas kernels: 41 us -> 39 us
  local copies, waits for them, and re-layouts: 2.8 us -> 1.24 us
    pallas_call x1, Pallas kernels: 41 us -> 39 us  [local(): pl.pallas_call(kernel, out_shape=(pltpu.VMEM((2, COLS, SLOTS), BF16), plt...]
    unnamed x2, local copies, waits for them, and re-layouts: 2.8 us -> 1.24 us
where the time goes in v3:
time: 41.3 us; the launch traced here: 40.9 us
  Pallas kernels  39 us (94%)
  local copies, waits for them, and re-layouts  1.24 us (3%)
  between operations  0.64 us (2%)
    pallas_call x1, Pallas kernels, local(): pl.pallas_call(kernel, out_shape=(pltpu.VMEM((2, COLS, SLOTS), BF16), plt...  39 us
    unnamed x2, local copies, waits for them, and re-layouts  1.24 us

profile of v3, /device:TPU:1, one launch (start us, length us, event | category | flops | bytes accessed | tf_op | source)
XLA Modules:
  0.0 40.9 jit_solution(6699669631476560710)
XLA Ops:
  0.6 39.0 %regroup_attend.1 = (bf16[2,192,256]{2,1,0:T(8,128)(2,1)S(1)}, bf16[2,192]{1,0:T(2,128)(2,1)S(1)}) custom-call(bf16[352,768]{1,0:T(8,128)(2,1)} %feat.1, bf16[768,768]{1,0:T(8,128)(2,1)} %w.1, f32[768]{0:T(1024)} %bias.1, bf16[192,768]{1,0:T(8,128)(2,1)} %bitcast.8, bf16[192,768]{1,0:T(8,128)(2,1)} %bitcast.9, bf16[192,768]{1,0:T(8,128)(2,1)} %bitcast.10, ...), custom_call_target="tpu_custom_call" | custom-call | tf_op jit(solution)/shard_map/regroup_attend/pallas_call | solution.py:277
  39.7 0.7 %copy.14 = bf16[2,256,192]{1,2,0:T(8,128)(2,1)} copy(bf16[2,256,192]{1,2,0:T(8,128)(2,1)S(1)} %bitcast.7) | data formatting | bytes 393216
  40.4 0.6 %copy.15 = bf16[2,192]{1,0:T(2,128)(2,1)} copy(bf16[2,192]{1,0:T(2,128)(2,1)S(1)} %get-tuple-element.7) | data formatting | bytes 1536

commit v4 on v3

--- a/solution.py
+++ b/solution.py
@@ -58,10 +58,11 @@
         pltpu.make_async_copy(wo, wo_v, in_sem.at[8]),
         pltpu.make_async_copy(cnt, cnt_v, in_sem.at[9]),
     ]
-    for load in loads:
-        load.start()
-
     barrier = pltpu.get_barrier_semaphore()
+    for o in (8, 7, 9, 6, 10, 5, 11, 4, 12, 3, 13, 2, 14, 1, 15):
+        pl.semaphore_signal(
+            barrier, inc=1, device_id={"dp": ((z + o) % NZ) * NG + g, "head": h}, device_id_type=MESH
+        )
     for o in range(NG):
         source = (g + o) % NG
         if o == 0:
@@ -74,14 +75,12 @@
             pl.semaphore_signal(
                 barrier, inc=1, device_id={"dp": z * NG + source, "head": y}, device_id_type=MESH
             )
-    for o in range(1, NZ):
-        pl.semaphore_signal(
-            barrier, inc=1, device_id={"dp": ((z + o) % NZ) * NG + g, "head": h}, device_id_type=MESH
-        )
     for o in range(1, NX):
         pl.semaphore_signal(
             barrier, inc=1, device_id={"dp": dp, "head": (h + o) % NX}, device_id_type=MESH
         )
+    for load in loads:
+        load.start()
 
     f_v[pl.ds(TILE, PAD - TILE), :] = jnp.zeros((PAD - TILE, D), BF16)
     upper = (iota((PAD, PAD), 0) < iota((PAD, PAD), 1)).astype(F32).astype(BF16)
@@ -191,6 +190,13 @@
         )
     size = 16 * CHUNK
     for n in range(CHUNKS):
+        if n == CHUNKS - 1:
+            for copy in z_sends.values():
+                copy.wait_send()
+            for copy in x_sends[:-7]:
+                copy.wait_send()
+            for copy in local_sends[:-1]:
+                pl.when(y != h)(copy.wait_send)
         for source in range(NG):
             landed = a_v.at[:, n, source]
             pltpu.make_async_copy(landed, landed, xr_sem.at[n, source]).wait()
@@ -253,12 +259,9 @@
         ordered = jnp.where(alive[j], perm_v[...].astype(F32), 0.0).astype(BF16)
         result = jnp.dot(mixed[j], ordered, preferred_element_type=F32)
         mixed_out[j] = result.astype(BF16)
-    for copy in z_sends.values():
+    for copy in x_sends[-7:]:
         copy.wait_send()
-    for copy in x_sends:
-        copy.wait_send()
-    for copy in local_sends:
-        pl.when(y != h)(copy.wait_send)
+    pl.when(y != h)(local_sends[-1].wait_send)
     own_part = s_v[h]
     for copy in p_sends:
         copy.wait_recv()

time: 41.3 us -> 41.2 us (level)
  no operation moved by 1% of the time
where the time goes in v4:
time: 41.2 us; the launch traced here: 40.6 us
  Pallas kernels  38.7 us (94%)
  local copies, waits for them, and re-layouts  1.24 us (3%)
  between operations  0.64 us (2%)
    pallas_call x1, Pallas kernels, local(): pl.pallas_call(kernel, out_shape=(pltpu.VMEM((2, COLS, SLOTS), BF16), plt...  38.7 us
    unnamed x2, local copies, waits for them, and re-layouts  1.24 us

profile of v4, /device:TPU:1, one launch (start us, length us, event | category | flops | bytes accessed | tf_op | source)
XLA Modules:
  0.0 40.6 jit_solution(8232346421305412456)
XLA Ops:
  0.6 38.7 %regroup_attend.1 = (bf16[2,192,256]{2,1,0:T(8,128)(2,1)S(1)}, bf16[2,192]{1,0:T(2,128)(2,1)S(1)}) custom-call(bf16[352,768]{1,0:T(8,128)(2,1)} %feat.1, bf16[768,768]{1,0:T(8,128)(2,1)} %w.1, f32[768]{0:T(1024)} %bias.1, bf16[192,768]{1,0:T(8,128)(2,1)} %bitcast.8, bf16[192,768]{1,0:T(8,128)(2,1)} %bitcast.9, bf16[192,768]{1,0:T(8,128)(2,1)} %bitcast.10, ...), custom_call_target="tpu_custom_call" | custom-call | tf_op jit(solution)/shard_map/regroup_attend/pallas_call | solution.py:280
  39.3 0.7 %copy.14 = bf16[2,256,192]{1,2,0:T(8,128)(2,1)} copy(bf16[2,256,192]{1,2,0:T(8,128)(2,1)S(1)} %bitcast.7) | data formatting | bytes 393216
  40.0 0.6 %copy.15 = bf16[2,192]{1,0:T(2,128)(2,1)} copy(bf16[2,192]{1,0:T(2,128)(2,1)S(1)} %get-tuple-element.7) | data formatting | bytes 1536

commit v5 on v4

--- a/solution.py
+++ b/solution.py
@@ -22,7 +22,7 @@
 CHUNK = 4
 CHUNKS = NZ // CHUNK
 OFFSETS = (0, 1, 15, 2, 14, 3, 13, 4, 12, 5, 11, 6, 10, 7, 9, 8)
-ISSUE = (1, 15, 2, 14, 3, 13, 4, 12, 5, 11, 6, 10, 7, 9, 8)
+DIRECT = (1, 15, 2, 14, 3, 13, 4, 12, 5, 11, 6, 10)
 
 
 def iota(shape, dim):
@@ -33,8 +33,8 @@
     feat, w, bias, wq, wk, wv, wo, reg, blk, cnt,
     mixed_out, region_out,
     f_v, w_v, bias_v, wq_v, wk_v, wv_v, wo_v, reg_v, blk_v, cnt_v,
-    e_v, z_v, c_v, a_v, q_v, k_v, perm_v, s_v, r_v,
-    in_sem, own_sem, zs_sem, zr_sem, xs_sem, xr_sem, ps_sem, pr_sem,
+    e_v, z_v, up_v, down_v, c_v, a_v, q_v, k_v, perm_v, s_v, r_v,
+    in_sem, own_sem, zs_sem, zr_sem, relay_sem, xs_sem, xr_sem, ps_sem, pr_sem,
 ):
     dp = lax.axis_index("dp")
     h = lax.axis_index("head")
@@ -59,7 +59,7 @@
         pltpu.make_async_copy(cnt, cnt_v, in_sem.at[9]),
     ]
     barrier = pltpu.get_barrier_semaphore()
-    for o in (8, 7, 9, 6, 10, 5, 11, 4, 12, 3, 13, 2, 14, 1, 15):
+    for o in reversed(DIRECT):
         pl.semaphore_signal(
             barrier, inc=1, device_id={"dp": ((z + o) % NZ) * NG + g, "head": h}, device_id_type=MESH
         )
@@ -102,7 +102,7 @@
     rank = jnp.sum(before * hot, axis=0, keepdims=True)
     code = jnp.where(in_range[0:1, :], block[0:1, :] * 2.0 + rank, -1.0)
     row = iota((128, PAD), 0)
-    target = (32 * (row // NG) + 8 * h + row % NG).astype(F32)
+    target = (32 * ((z + row // NG) % NZ) + 8 * h + row % NG).astype(F32)
     pick = (code == target).astype(F32)
     live = jnp.sum(pick, axis=1, keepdims=True)
     loads[2].wait()
@@ -114,23 +114,27 @@
     embedded = jnp.where(live > 0.5, embedded, EMPTY).astype(BF16)
     e_v[...] = embedded.reshape(NZ, NG, D)
 
-    pl.semaphore_wait(barrier, NG + NZ - 1 + NX - 1 - (y == h).astype(jnp.int32))
-
+    pl.semaphore_wait(barrier, NG + len(DIRECT) + NX - 1 - (y == h).astype(jnp.int32))
+
+    def along_z(source, target, away, sent, got):
+        copy = pltpu.make_async_remote_copy(
+            src_ref=source,
+            dst_ref=target,
+            send_sem=zs_sem.at[sent],
+            recv_sem=got,
+            device_id={"dp": ((z + away) % NZ) * NG + g, "head": h},
+            device_id_type=MESH,
+        )
+        copy.start()
+        return copy
+
+    up = along_z(e_v.at[pl.ds(7, 2)], up_v, 3, 0, relay_sem.at[0])
+    down = along_z(e_v.at[pl.ds(9, 1)], down_v, 13, NZ, relay_sem.at[1])
     z_sends = {}
-    for offset in ISSUE:
-        p = OFFSETS.index(offset)
-        to = (z + NZ - offset) % NZ
-        copy = pltpu.make_async_remote_copy(
-            src_ref=e_v.at[to],
-            dst_ref=z_v.at[p],
-            send_sem=zs_sem.at[p],
-            recv_sem=zr_sem.at[p],
-            device_id={"dp": to * NG + g, "head": h},
-            device_id_type=MESH,
-        )
-        copy.start()
-        z_sends[p] = copy
-    own = pltpu.make_async_copy(e_v.at[z], z_v.at[0], own_sem)
+    for k in DIRECT:
+        p = OFFSETS.index(NZ - k)
+        z_sends[p] = along_z(e_v.at[k], z_v.at[p], k, p, zr_sem.at[p])
+    own = pltpu.make_async_copy(e_v.at[0], z_v.at[0], own_sem)
     own.start()
 
     at = iota((SLOTS, SLOTS), 0)
@@ -146,6 +150,12 @@
     out_row = iota((rows, rows), 0)
     in_row = (out_row % CHUNK) * 8 + out_row // 8 % 2 * 2 + out_row // 16 * 4 + out_row // CHUNK % 2
     order = (iota((rows, rows), 1) == in_row).astype(F32).astype(BF16)
+    up.wait_recv()
+    down.wait_recv()
+    for source, away, offset in ((up_v.at[1], 5, 8), (up_v.at[0], 4, 9), (down_v.at[0], 12, 7)):
+        p = OFFSETS.index(offset)
+        z_sends[p] = along_z(source, z_v.at[p], away, p, zr_sem.at[p])
+
     x_sends = []
     local_sends = []
     for n in range(CHUNKS):
@@ -191,7 +201,7 @@
     size = 16 * CHUNK
     for n in range(CHUNKS):
         if n == CHUNKS - 1:
-            for copy in z_sends.values():
+            for copy in (up, down, *z_sends.values()):
                 copy.wait_send()
             for copy in x_sends[:-7]:
                 copy.wait_send()
@@ -298,6 +308,8 @@
             pltpu.VMEM((1, 256), jnp.int32),
             pltpu.VMEM((NZ, NG, D), BF16),
             pltpu.VMEM((NZ, NG, D), BF16),
+            pltpu.VMEM((2, NG, D), BF16),
+            pltpu.VMEM((1, NG, D), BF16),
             pltpu.VMEM((CHUNKS, 2, 2, 2 * CHUNK, D), BF16),
             pltpu.VMEM((2, CHUNKS, NG, 2 * CHUNK, D), BF16),
             pltpu.VMEM((2, SLOTS, COLS), BF16),
@@ -307,8 +319,9 @@
             pltpu.VMEM((NX - 1, 8, 256), F32),
             dma((10,)),
             dma,
+            dma((NZ + 1,)),
             dma((NZ,)),
-            dma((NZ,)),
+            dma((2,)),
             dma((CHUNKS, NX, 2)),
             dma((CHUNKS, NG)),
             dma((NX - 1,)),

time: 41.2 us -> 40.8 us (level); the launches traced: 40.6 us -> 40.6 us
  no operation moved by 1% of the time
where the time goes in v5:
time: 40.8 us; the launch traced here: 40.6 us
  Pallas kernels  38.7 us (95%)
  local copies, waits for them, and re-layouts  1.24 us (3%)
  between operations  0.64 us (2%)
    pallas_call x1, Pallas kernels, local(): pl.pallas_call(kernel, out_shape=(pltpu.VMEM((2, COLS, SLOTS), BF16), plt...  38.7 us
    unnamed x2, local copies, waits for them, and re-layouts  1.24 us

profile of v5, /device:TPU:1, one launch (start us, length us, event | category | flops | bytes accessed | tf_op | source)
XLA Modules:
  0.0 40.6 jit_solution(17864796786912434706)
XLA Ops:
  0.6 38.7 %regroup_attend.1 = (bf16[2,192,256]{2,1,0:T(8,128)(2,1)S(1)}, bf16[2,192]{1,0:T(2,128)(2,1)S(1)}) custom-call(bf16[352,768]{1,0:T(8,128)(2,1)} %feat.1, bf16[768,768]{1,0:T(8,128)(2,1)} %w.1, f32[768]{0:T(1024)} %bias.1, bf16[192,768]{1,0:T(8,128)(2,1)} %bitcast.8, bf16[192,768]{1,0:T(8,128)(2,1)} %bitcast.9, bf16[192,768]{1,0:T(8,128)(2,1)} %bitcast.10, ...), custom_call_target="tpu_custom_call" | custom-call | tf_op jit(solution)/shard_map/regroup_attend/pallas_call | solution.py:290
  39.4 0.7 %copy.14 = bf16[2,256,192]{1,2,0:T(8,128)(2,1)} copy(bf16[2,256,192]{1,2,0:T(8,128)(2,1)S(1)} %bitcast.7) | data formatting | bytes 393216
  40.1 0.6 %copy.15 = bf16[2,192]{1,0:T(2,128)(2,1)} copy(bf16[2,192]{1,0:T(2,128)(2,1)S(1)} %get-tuple-element.7) | data formatting | bytes 1536

commit v6 on v5

--- a/solution.py
+++ b/solution.py
@@ -150,15 +150,15 @@
     out_row = iota((rows, rows), 0)
     in_row = (out_row % CHUNK) * 8 + out_row // 8 % 2 * 2 + out_row // 16 * 4 + out_row // CHUNK % 2
     order = (iota((rows, rows), 1) == in_row).astype(F32).astype(BF16)
-    up.wait_recv()
-    down.wait_recv()
-    for source, away, offset in ((up_v.at[1], 5, 8), (up_v.at[0], 4, 9), (down_v.at[0], 12, 7)):
-        p = OFFSETS.index(offset)
-        z_sends[p] = along_z(source, z_v.at[p], away, p, zr_sem.at[p])
-
     x_sends = []
     local_sends = []
     for n in range(CHUNKS):
+        if n == 1:
+            up.wait_recv()
+            down.wait_recv()
+            for source, away, offset in ((up_v.at[1], 5, 8), (up_v.at[0], 4, 9), (down_v.at[0], 12, 7)):
+                p = OFFSETS.index(offset)
+                z_sends[p] = along_z(source, z_v.at[p], away, p, zr_sem.at[p])
         for p in range(n * CHUNK, (n + 1) * CHUNK):
             if p == 0:
                 own.wait()
@@ -215,7 +215,6 @@
             made = lax.dot_general(rows, weight[...], LAST, preferred_element_type=F32)
             kept[:, n * size : (n + 1) * size] = made.astype(BF16).reshape(2, size, COLS)
 
-    lane = iota((SLOTS, COLS), 1)
     first = (iota((8, 128), 1) == 0).astype(F32).astype(BF16)
     pairs = [(j, n) for j in range(2) for n in range(3)]
     alive, alive_row, scores, vals = [], [], {}, []
@@ -225,10 +224,10 @@
         mark = lax.dot_general(first, marks, LAST, preferred_element_type=F32)
         alive_row.append((mark > -4.0).astype(F32).astype(BF16))
     for j, n in pairs:
-        keys = k_v[j]
-        mine = (lane >= n * HD) & (lane < (n + 1) * HD)
-        head_keys = jnp.where(mine, keys, jnp.zeros_like(keys))
-        scores[j, n] = lax.dot_general(head_keys, q_v[j], LAST, preferred_element_type=F32)
+        scores[j, n] = lax.dot_general(
+            k_v[j, :, n * HD : (n + 1) * HD], q_v[j, :, n * HD : (n + 1) * HD], LAST,
+            preferred_element_type=F32,
+        )
     for j in range(2):
         rows = a_v[j].reshape(SLOTS, D)
         made = lax.dot_general(wv_v[...], rows, LAST, preferred_element_type=F32)

time: 40.8 us -> 40.8 us (level)
  no operation moved by 1% of the time
where the time goes in v6:
time: 40.8 us; the launch traced here: 40.6 us
  Pallas kernels  38.7 us (95%)
  local copies, waits for them, and re-layouts  1.24 us (3%)
  between operations  0.64 us (2%)
    pallas_call x1, Pallas kernels, local(): pl.pallas_call(kernel, out_shape=(pltpu.VMEM((2, COLS, SLOTS), BF16), plt...  38.7 us
    unnamed x2, local copies, waits for them, and re-layouts  1.24 us

profile of v6, /device:TPU:1, one launch (start us, length us, event | category | flops | bytes accessed | tf_op | source)
XLA Modules:
  0.0 40.6 jit_solution(17035272695360926193)
XLA Ops:
  0.6 38.7 %regroup_attend.1 = (bf16[2,192,256]{2,1,0:T(8,128)(2,1)S(1)}, bf16[2,192]{1,0:T(2,128)(2,1)S(1)}) custom-call(bf16[352,768]{1,0:T(8,128)(2,1)} %feat.1, bf16[768,768]{1,0:T(8,128)(2,1)} %w.1, f32[768]{0:T(1024)} %bias.1, bf16[192,768]{1,0:T(8,128)(2,1)} %bitcast.8, bf16[192,768]{1,0:T(8,128)(2,1)} %bitcast.9, bf16[192,768]{1,0:T(8,128)(2,1)} %bitcast.10, ...), custom_call_target="tpu_custom_call" | custom-call | tf_op jit(solution)/shard_map/regroup_attend/pallas_call | solution.py:289
  39.3 0.7 %copy.14 = bf16[2,256,192]{1,2,0:T(8,128)(2,1)} copy(bf16[2,256,192]{1,2,0:T(8,128)(2,1)S(1)} %bitcast.7) | data formatting | bytes 393216
  40.0 0.6 %copy.15 = bf16[2,192]{1,0:T(2,128)(2,1)} copy(bf16[2,192]{1,0:T(2,128)(2,1)S(1)} %get-tuple-element.7) | data formatting | bytes 1536

commit v7 on v6

--- a/solution.py
+++ b/solution.py
@@ -22,7 +22,7 @@
 CHUNK = 4
 CHUNKS = NZ // CHUNK
 OFFSETS = (0, 1, 15, 2, 14, 3, 13, 4, 12, 5, 11, 6, 10, 7, 9, 8)
-DIRECT = (1, 15, 2, 14, 3, 13, 4, 12, 5, 11, 6, 10)
+DIRECT = (1, 15, 2, 14, 3, 13, 4, 12, 5, 11)
 
 
 def iota(shape, dim):
@@ -128,8 +128,8 @@
         copy.start()
         return copy
 
-    up = along_z(e_v.at[pl.ds(7, 2)], up_v, 3, 0, relay_sem.at[0])
-    down = along_z(e_v.at[pl.ds(9, 1)], down_v, 13, NZ, relay_sem.at[1])
+    up = along_z(e_v.at[pl.ds(6, 3)], up_v, 3, 0, relay_sem.at[0])
+    down = along_z(e_v.at[pl.ds(9, 2)], down_v, 13, NZ, relay_sem.at[1])
     z_sends = {}
     for k in DIRECT:
         p = OFFSETS.index(NZ - k)
@@ -156,7 +156,7 @@
         if n == 1:
             up.wait_recv()
             down.wait_recv()
-            for source, away, offset in ((up_v.at[1], 5, 8), (up_v.at[0], 4, 9), (down_v.at[0], 12, 7)):
+            for source, away, offset in ((up_v.at[2], 5, 8), (up_v.at[1], 4, 9), (up_v.at[0], 3, 10), (down_v.at[0], 12, 7), (down_v.at[1], 13, 6)):
                 p = OFFSETS.index(offset)
                 z_sends[p] = along_z(source, z_v.at[p], away, p, zr_sem.at[p])
         for p in range(n * CHUNK, (n + 1) * CHUNK):
@@ -307,8 +307,8 @@
             pltpu.VMEM((1, 256), jnp.int32),
             pltpu.VMEM((NZ, NG, D), BF16),
             pltpu.VMEM((NZ, NG, D), BF16),
+            pltpu.VMEM((3, NG, D), BF16),
             pltpu.VMEM((2, NG, D), BF16),
-            pltpu.VMEM((1, NG, D), BF16),
             pltpu.VMEM((CHUNKS, 2, 2, 2 * CHUNK, D), BF16),
             pltpu.VMEM((2, CHUNKS, NG, 2 * CHUNK, D), BF16),
             pltpu.VMEM((2, SLOTS, COLS), BF16),

time: 40.8 us -> 40.7 us (level)
  no operation moved by 1% of the time
where the time goes in v7:
time: 40.7 us; the launch traced here: 40.5 us
  Pallas kernels  38.7 us (95%)
  local copies, waits for them, and re-layouts  1.24 us (3%)
  between operations  0.64 us (2%)
    pallas_call x1, Pallas kernels, local(): pl.pallas_call(kernel, out_shape=(pltpu.VMEM((2, COLS, SLOTS), BF16), plt...  38.7 us
    unnamed x2, local copies, waits for them, and re-layouts  1.24 us

profile of v7, /device:TPU:1, one launch (start us, length us, event | category | flops | bytes accessed | tf_op | source)
XLA Modules:
  0.0 40.5 jit_solution(12662172746482980906)
XLA Ops:
  0.6 38.7 %regroup_attend.1 = (bf16[2,192,256]{2,1,0:T(8,128)(2,1)S(1)}, bf16[2,192]{1,0:T(2,128)(2,1)S(1)}) custom-call(bf16[352,768]{1,0:T(8,128)(2,1)} %feat.1, bf16[768,768]{1,0:T(8,128)(2,1)} %w.1, f32[768]{0:T(1024)} %bias.1, bf16[192,768]{1,0:T(8,128)(2,1)} %bitcast.8, bf16[192,768]{1,0:T(8,128)(2,1)} %bitcast.9, bf16[192,768]{1,0:T(8,128)(2,1)} %bitcast.10, ...), custom_call_target="tpu_custom_call" | custom-call | tf_op jit(solution)/shard_map/regroup_attend/pallas_call | solution.py:289
  39.3 0.7 %copy.14 = bf16[2,256,192]{1,2,0:T(8,128)(2,1)} copy(bf16[2,256,192]{1,2,0:T(8,128)(2,1)S(1)} %bitcast.7) | data formatting | bytes 393216
  40.0 0.6 %copy.15 = bf16[2,192]{1,0:T(2,128)(2,1)} copy(bf16[2,192]{1,0:T(2,128)(2,1)S(1)} %get-tuple-element.7) | data formatting | bytes 1536
